TPU v7x, 512 devices: a whole 4x8x8 slice. The times are simulated.
512 devices in a mesh: rows: 16 (over z, core), rhs: 32 (over y, x).
Axes of the slice: x: 4, y: 8, z: 8, core: 2. Of those that a mesh axis runs over, the one named last changes fastest.
Arguments:
- rhs_blocks: bfloat16 [16, 2048, 4096], P('rows', None, 'rhs'), may hold values from -6 to 6
- left_u: bfloat16 [16, 4, 2048, 256], P('rows', None, 'rhs'), may hold values from -0.375 to 0.375
- left_v: bfloat16 [16, 4, 2048, 256], P('rows', None, 'rhs'), may hold values from -0.125 to 0.125
- tile_ranks: int32 [16, 4], P('rows'), may hold values from 32 to 256
- diag_inverse: bfloat16 [4, 2048, 2048], P(None, 'rows'), may hold values from -8 to 8, as said below
- row_owner: int32 [16], replicated, may hold values from 0 to 15, each once
Outputs:
- solved: bfloat16 [4, 2048, 4096], P(None, 'rows', 'rhs')
- updated: bfloat16 [16, 2048, 4096], P('rows', None, 'rhs')
Inputs may be any that keep to these rules, and one draw needn't show every extreme that they name: tile_ranks[s, k] is the rank of the tile in column k of the tile row stored in block s. row_owner[s] is the tile row held in stored block s; every tile row is held exactly once. Each diag_inverse[k] is lower triangular.
All inputs are finite; a program needn't handle non-finite values.
Results may differ from a plain program's by a relative error of at most 0.01.
Values may be sent and summed in bfloat16 or wider, within the bound.
A program may use at most 64 MiB of HBM per device.

v0:
```python
import jax
import jax.numpy as jnp
from jax import lax
from jax.sharding import PartitionSpec as P


def sent_together(arrays, axis, dim, along):
    both = jnp.concatenate(arrays, axis=along)
    filled, at, outs = (lax.all_gather(both, axis, axis=dim, tiled=True), 0, [])
    for a in arrays:
        outs.append(lax.slice_in_dim(filled, at, at + a.shape[along], axis=along))
        at += a.shape[along]
    return tuple(outs)


def cut_along(array, dim, peers):
    before, after = (array.shape[:dim], array.shape[dim + 1 :])
    return jnp.moveaxis(array.reshape(*before, peers, -1, *after), dim, 0)


def sent_and_summed(array, axis, dim):
    blocks = cut_along(array, dim, lax.axis_size(axis))
    arrived = lax.all_to_all(blocks, axis, split_axis=0, concat_axis=0, tiled=True)
    return arrived.astype(jnp.float32).sum(axis=0)


def copy_for_each(array, axis):
    peers = lax.axis_size(axis)
    return lax.all_to_all(
        jnp.broadcast_to(array[None], (peers, *array.shape)), axis, 0, 0, tiled=True
    )


def joined_along(blocks, dim):
    blocks = jnp.moveaxis(blocks, 0, dim)
    lengths = blocks.shape
    return blocks.reshape(*lengths[:dim], lengths[dim] * lengths[dim + 1], *lengths[dim + 2 :])


def gather_directly(array, axis, dim):
    blocks = copy_for_each(array, axis)
    return joined_along(blocks, dim)


def left_product(v_piece, x_rows, tile_rank):
    width = v_piece.shape[1]
    keep_cols = (jnp.arange(width, dtype=jnp.int32) < tile_rank).astype(v_piece.dtype)
    dims = (((0,), (0,)), ((), ()))
    return lax.dot_general(v_piece * keep_cols, x_rows, dims, preferred_element_type=jnp.float32)


def right_product(u_piece, coeffs):
    return jnp.dot(u_piece, coeffs, preferred_element_type=jnp.float32)


def body(rhs_blocks, left_u, left_v, tile_ranks, diag_inverse, row_owner):
    my_index = lax.axis_index("rows")
    stored = jnp.arange(row_owner.shape[0], dtype=jnp.int32)
    my_row = jnp.sum(jnp.where(stored == my_index, row_owner, 0))
    residual = rhs_blocks[0].astype(jnp.float32)
    u_whole, v_whole = sent_together((left_u[0], left_v[0]), "rhs", 1, 0)
    solved_parts = []
    for column in range(diag_inverse.shape[0]):
        owner_index = jnp.sum(jnp.where(row_owner == column, stored, 0))
        inverse_rows = diag_inverse[column]
        rounded = residual.astype(jnp.bfloat16).astype(jnp.float32)
        offered = jnp.where(my_index == owner_index, rounded, jnp.zeros_like(rounded))
        own_piece = sent_and_summed(offered.astype(jnp.bfloat16), "rows", 0).astype(jnp.bfloat16)
        solved_part = jnp.dot(
            inverse_rows, gather_directly(own_piece, "rows", 0), preferred_element_type=jnp.float32
        ).astype(jnp.bfloat16)
        solved_parts.append(solved_part)
        solution = lax.all_gather(solved_part, "rows", axis=0, tiled=True)
        tile_rank = tile_ranks[0, column]
        coeffs = left_product(v_whole[column], solution, tile_rank).astype(jnp.bfloat16)
        update = right_product(u_whole[column], coeffs)
        residual = jnp.where(column < my_row, residual - update, residual)
    return (jnp.stack(solved_parts), residual.astype(jnp.bfloat16)[None])


def solution(mesh):
    return jax.shard_map(
        body,
        mesh=mesh,
        in_specs=(
            P("rows", None, "rhs"),
            P("rows", None, "rhs", None),
            P("rows", None, "rhs", None),
            P("rows", None),
            P(None, "rows", None),
            P(),
        ),
        out_specs=(P(None, "rows", "rhs"), P("rows", None, "rhs")),
        check_vma=False,
    )
```

profile of v0, /device:TPU:1, one launch (start us, length us, event | category | flops | bytes accessed | tf_op | source)
XLA Modules:
  0.0 326.2 jit_solution(11512626991886420572)
XLA Ops:
  7.2 1.8 pad_maximum_fusion
  9.1 1.4 fusion.40
  12.3 28.9 %all_to_all.40 = bf16[16,128,128]{2,1,0:T(8,128)(2,1)S(1)} all-to-all(bf16[16,128,128]{2,1,0:T(8,128)(2,1)S(1)} %bitcast.101), channel_id=1, replica_groups=mesh['rows'=16,'rhs'=32] {'rows'}, dimensions={0} | all-to-all | bytes 1048576 | tf_op jit(solution)/shard_map/all_to_all | solution.py:23
  42.2 3.5 %all-to-all-start.1 = ((bf16[16,128,128]{2,1,0:T(8,128)(2,1)}), bf16[16,128,128]{2,1,0:T(8,128)(2,1)S(1)}, u32[]{:S(2)}, u32[]{:S(2)}) async-start(bf16[16,128,128]{2,1,0:T(8,128)(2,1)} %broadcast_in_dim.16), calls=%async_computation.1 | async-start | bytes 1048576 | tf_op jit(solution)/shard_map/all_to_all | solution.py:29
  47.0 1.5 fusion.41
  49.1 13.3 %all-to-all-done.1 = bf16[16,128,128]{2,1,0:T(8,128)(2,1)S(1)} async-done(((bf16[16,128,128]{2,1,0:T(8,128)(2,1)}), bf16[16,128,128]{2,1,0:T(8,128)(2,1)S(1)}, u32[]{:S(2)}, u32[]{:S(2)}) %all-to-all-start.1) | async-done | bytes 524320 | tf_op jit(solution)/shard_map/all_to_all | solution.py:29
  63.8 15.9 %all_gather.16 = bf16[2048,128]{0,1:T(8,128)(2,1)S(1)} all-gather(bf16[128,128]{0,1:T(8,128)(2,1)S(1)} %bitcast.111), channel_id=1, replica_groups=mesh['rows'=16,'rhs'=32] {'rows'}, dimensions={0}, use_global_device_ids=true | all-gather | bytes 557056 | tf_op jit(solution)/shard_map/all_gather | solution.py:73
  79.7 39.9 %all-gather.2.cloned.1.call-done = bf16[8,2048,256]{2,1,0:T(8,128)(2,1)} async-done(((bf16[8,64,256]{2,1,0:T(8,128)(2,1)}), bf16[8,2048,256]{2,1,0:T(8,128)(2,1)}) %all-gather.2.cloned.1.call-update) | async-done | bytes 8388624 | tf_op jit(solution)/shard_map/all_gather | solution.py:9
  119.6 4.1 %select_convert_fusion.2 = (bf16[2048,128]{1,0:T(8,128)(2,1)S(1)}, f32[2048,128]{1,0:T(8,128)}) fusion(pred[]{:T(512)S(6)} %eq.33, bf16[2048,128]{0,1:T(8,128)(2,1)S(1)} %all_gather.16, bf16[8,2048,256]{2,1,0:T(8,128)(2,1)} %all-gather.2.cloned.1.call-done, bf16[256]{0:T(256)(128)(2,1)S(1)} %compare_convert_fusion.3, bf16[1,2048,128]{2,1,0:T(8,128)(2,1)} %param.6, ...), kind=kOutput, calls=%fused_computation.35 | convolution fusion | flops 270827520 | bytes 4719106 | tf_op jit(solution)/shard_map/dot_general | solution.py:53
  123.7 25.6 %all_to_all.41 = bf16[16,128,128]{2,1,0:T(8,128)(2,1)S(1)} all-to-all(bf16[16,128,128]{2,1,0:T(8,128)(2,1)S(1)} %bitcast.108), channel_id=1, replica_groups=mesh['rows'=16,'rhs'=32] {'rows'}, dimensions={0} | all-to-all | bytes 1048576 | tf_op jit(solution)/shard_map/all_to_all | solution.py:23
  150.3 3.5 %all-to-all-start.3 = ((bf16[16,128,128]{2,1,0:T(8,128)(2,1)}), bf16[16,128,128]{2,1,0:T(8,128)(2,1)S(1)}, u32[]{:S(2)}, u32[]{:S(2)}) async-start(bf16[16,128,128]{2,1,0:T(8,128)(2,1)} %broadcast_in_dim.17), calls=%async_computation.3 | async-start | bytes 1048576 | tf_op jit(solution)/shard_map/all_to_all | solution.py:29
  155.7 14.7 %all-to-all-done.3 = bf16[16,128,128]{2,1,0:T(8,128)(2,1)S(1)} async-done(((bf16[16,128,128]{2,1,0:T(8,128)(2,1)}), bf16[16,128,128]{2,1,0:T(8,128)(2,1)S(1)}, u32[]{:S(2)}, u32[]{:S(2)}) %all-to-all-start.3) | async-done | bytes 524320 | tf_op jit(solution)/shard_map/all_to_all | solution.py:29
  170.8 15.9 %all_gather.17 = bf16[2048,128]{0,1:T(8,128)(2,1)S(1)} all-gather(bf16[128,128]{0,1:T(8,128)(2,1)S(1)} %bitcast.113), channel_id=1, replica_groups=mesh['rows'=16,'rhs'=32] {'rows'}, dimensions={0}, use_global_device_ids=true | all-gather | bytes 557056 | tf_op jit(solution)/shard_map/all_gather | solution.py:73
  186.7 4.2 %select_convert_fusion.1 = (bf16[2048,128]{1,0:T(8,128)(2,1)S(1)}, f32[2048,128]{1,0:T(8,128)}) fusion(pred[]{:T(512)S(6)} %eq.37, f32[2048,128]{1,0:T(8,128)} %get-tuple-element.14, bf16[2048,128]{0,1:T(8,128)(2,1)S(1)} %all_gather.17, bf16[8,2048,256]{2,1,0:T(8,128)(2,1)} %all-gather.2.cloned.1.call-done, bf16[256]{0:T(256)(128)(2,1)S(1)} %compare_convert_fusion.2, ...), kind=kOutput, calls=%fused_computation.34 | convolution fusion | flops 270565376 | bytes 5243394 | tf_op jit(solution)/shard_map/dot_general | solution.py:53
  190.9 22.3 %all_to_all.42 = bf16[16,128,128]{2,1,0:T(8,128)(2,1)S(1)} all-to-all(bf16[16,128,128]{2,1,0:T(8,128)(2,1)S(1)} %bitcast.106), channel_id=1, replica_groups=mesh['rows'=16,'rhs'=32] {'rows'}, dimensions={0} | all-to-all | bytes 1048576 | tf_op jit(solution)/shard_map/all_to_all | solution.py:23
  214.2 3.5 %all-to-all-start.5 = ((bf16[16,128,128]{2,1,0:T(8,128)(2,1)}), bf16[16,128,128]{2,1,0:T(8,128)(2,1)S(1)}, u32[]{:S(2)}, u32[]{:S(2)}) async-start(bf16[16,128,128]{2,1,0:T(8,128)(2,1)} %broadcast_in_dim.18), calls=%async_computation.5 | async-start | bytes 1048576 | tf_op jit(solution)/shard_map/all_to_all | solution.py:29
  219.6 14.7 %all-to-all-done.5 = bf16[16,128,128]{2,1,0:T(8,128)(2,1)S(1)} async-done(((bf16[16,128,128]{2,1,0:T(8,128)(2,1)}), bf16[16,128,128]{2,1,0:T(8,128)(2,1)S(1)}, u32[]{:S(2)}, u32[]{:S(2)}) %all-to-all-start.5) | async-done | bytes 524320 | tf_op jit(solution)/shard_map/all_to_all | solution.py:29
  234.7 15.9 %all_gather.18 = bf16[2048,128]{0,1:T(8,128)(2,1)S(1)} all-gather(bf16[128,128]{0,1:T(8,128)(2,1)S(1)} %bitcast.115), channel_id=1, replica_groups=mesh['rows'=16,'rhs'=32] {'rows'}, dimensions={0}, use_global_device_ids=true | all-gather | bytes 557056 | tf_op jit(solution)/shard_map/all_gather | solution.py:73
  250.6 4.3 %select_convert_fusion = (bf16[2048,128]{1,0:T(8,128)(2,1)S(1)}, f32[2048,128]{1,0:T(8,128)}) fusion(pred[]{:T(512)S(6)} %eq.39, f32[2048,128]{1,0:T(8,128)} %get-tuple-element.16, bf16[2048,128]{0,1:T(8,128)(2,1)S(1)} %all_gather.18, bf16[8,2048,256]{2,1,0:T(8,128)(2,1)} %all-gather.2.cloned.1.call-done, bf16[256]{0:T(256)(128)(2,1)S(1)} %compare_convert_fusion.1, ...), kind=kOutput, calls=%fused_computation.33 | convolution fusion | flops 270565376 | bytes 5243394 | tf_op jit(solution)/shard_map/dot_general | solution.py:53
  254.9 22.3 %all_to_all.43 = bf16[16,128,128]{2,1,0:T(8,128)(2,1)S(1)} all-to-all(bf16[16,128,128]{2,1,0:T(8,128)(2,1)S(1)} %bitcast.107), channel_id=1, replica_groups=mesh['rows'=16,'rhs'=32] {'rows'}, dimensions={0} | all-to-all | bytes 1048576 | tf_op jit(solution)/shard_map/all_to_all | solution.py:23
  278.2 3.5 %all-to-all-start.7 = ((bf16[16,128,128]{2,1,0:T(8,128)(2,1)}), bf16[16,128,128]{2,1,0:T(8,128)(2,1)S(1)}, u32[]{:S(2)}, u32[]{:S(2)}) async-start(bf16[16,128,128]{2,1,0:T(8,128)(2,1)} %broadcast_in_dim.19), calls=%async_computation.7 | async-start | bytes 1048576 | tf_op jit(solution)/shard_map/all_to_all | solution.py:29
  282.9 15.5 %all-to-all-done.7 = bf16[16,128,128]{2,1,0:T(8,128)(2,1)S(1)} async-done(((bf16[16,128,128]{2,1,0:T(8,128)(2,1)}), bf16[16,128,128]{2,1,0:T(8,128)(2,1)S(1)}, u32[]{:S(2)}, u32[]{:S(2)}) %all-to-all-start.7) | async-done | bytes 524320 | tf_op jit(solution)/shard_map/all_to_all | solution.py:29
  299.5 15.9 %all_gather.19 = bf16[2048,128]{0,1:T(8,128)(2,1)S(1)} all-gather(bf16[128,128]{0,1:T(8,128)(2,1)S(1)} %bitcast.118), channel_id=1, replica_groups=mesh['rows'=16,'rhs'=32] {'rows'}, dimensions={0}, use_global_device_ids=true | all-gather | bytes 557056 | tf_op jit(solution)/shard_map/all_gather | solution.py:73
  315.4 4.0 %fusion.5 = bf16[1,2048,128]{2,1,0:T(8,128)(2,1)} fusion(f32[2048,128]{1,0:T(8,128)} %get-tuple-element.18, bf16[8,2048,256]{2,1,0:T(8,128)(2,1)} %all-gather.2.cloned.1.call-done, bf16[2048,128]{0,1:T(8,128)(2,1)S(1)} %all_gather.19, bf16[256]{0:T(256)(128)(2,1)S(1)} %compare_convert_fusion, pred[]{:T(512)S(6)} %gt.15), kind=kOutput, calls=%fused_computation.9 | convolution fusion | flops 269778944 | bytes 4194817 | tf_op jit(solution)/shard_map/dot_general | solution.py:53
  (23 shorter events, 10.8 us)
Async XLA Ops:
  7.2 163.3 %copy-start = (bf16[4,128,2048]{2,1,0:T(8,128)(2,1)S(1)}, bf16[4,128,2048]{2,1,0:T(8,128)(2,1)}, u32[]{:S(2)}) copy-start(bf16[4,128,2048]{2,1,0:T(8,128)(2,1)} %param.10) | copy-start | bytes 6291460
  7.2 112.4 %all-gather.2.cloned.1.call-start = ((), (), s32[]{:S(2)}) async-start(), calls=%async_computation.8 | async-start | bytes 8650752 | tf_op jit(solution)/shard_map/all_gather | solution.py:9
  42.2 20.2 %all-to-all-start.1 = ((bf16[16,128,128]{2,1,0:T(8,128)(2,1)}), bf16[16,128,128]{2,1,0:T(8,128)(2,1)S(1)}, u32[]{:S(2)}, u32[]{:S(2)}) async-start(bf16[16,128,128]{2,1,0:T(8,128)(2,1)} %broadcast_in_dim.16), calls=%async_computation.1 | async-start | bytes 1048576 | tf_op jit(solution)/shard_map/all_to_all | solution.py:29
  150.3 20.2 %all-to-all-start.3 = ((bf16[16,128,128]{2,1,0:T(8,128)(2,1)}), bf16[16,128,128]{2,1,0:T(8,128)(2,1)S(1)}, u32[]{:S(2)}, u32[]{:S(2)}) async-start(bf16[16,128,128]{2,1,0:T(8,128)(2,1)} %broadcast_in_dim.17), calls=%async_computation.3 | async-start | bytes 1048576 | tf_op jit(solution)/shard_map/all_to_all | solution.py:29
  214.2 20.2 %all-to-all-start.5 = ((bf16[16,128,128]{2,1,0:T(8,128)(2,1)}), bf16[16,128,128]{2,1,0:T(8,128)(2,1)S(1)}, u32[]{:S(2)}, u32[]{:S(2)}) async-start(bf16[16,128,128]{2,1,0:T(8,128)(2,1)} %broadcast_in_dim.18), calls=%async_computation.5 | async-start | bytes 1048576 | tf_op jit(solution)/shard_map/all_to_all | solution.py:29
  278.2 20.2 %all-to-all-start.7 = ((bf16[16,128,128]{2,1,0:T(8,128)(2,1)}), bf16[16,128,128]{2,1,0:T(8,128)(2,1)S(1)}, u32[]{:S(2)}, u32[]{:S(2)}) async-start(bf16[16,128,128]{2,1,0:T(8,128)(2,1)} %broadcast_in_dim.19), calls=%async_computation.7 | async-start | bytes 1048576 | tf_op jit(solution)/shard_map/all_to_all | solution.py:29
Sparse Core Ops, SparseCore 0:
  11.2 108.3 all-gather.1
where the time goes:
time: 327 us; the launch traced here: 326 us
  blocking collectives  163 us (50%)
  waiting for transfers between devices  98.1 us (30%)
  between operations  19.4 us (6%)
  matrix products  19.1 us (6%)
  starting transfers between devices  13.9 us (4%)
  other arithmetic  7.26 us (2%)
  local copies, waits for them, and re-layouts  5.82 us (2%)
    all_to_all x4, blocking collectives, sent_and_summed(): lax.all_to_all(blocks, axis, split_axis=0, concat_axis=0, tiled=True)  99.1 us
    all_gather x4, blocking collectives, body(): solution = lax.all_gather(solved_part, 'rows', axis=0, tiled=True)  63.6 us
    all_to_all x4, waiting for transfers between devices, copy_for_each(): lax.all_to_all(jnp.broadcast_to(array[None], (peers, *array.shape)), axis...  58.2 us
    all_gather x1, waiting for transfers between devices, sent_together(): filled, at, outs = (lax.all_gather(both, axis, axis=dim, tiled=True), 0, [])  39.9 us
    dot_general x4, matrix products, right_product(): return jnp.dot(u_piece, coeffs, preferred_element_type=jnp.float32)  16.7 us
    all_to_all x4, starting transfers between devices, copy_for_each(): lax.all_to_all(jnp.broadcast_to(array[None], (peers, *array.shape)), axis...  13.9 us
  transfers between devices with their start and end apart: 5, of which 5 were waited for; matrix products, arithmetic and copies ran while one was open for 3% of the time, Pallas kernels for 0%

commit v1 on v0

v1 whole, which is shorter than its diff:
```python
import jax
import jax.numpy as jnp
from jax import lax
from jax.experimental import pallas as pl
from jax.experimental.pallas import tpu as pltpu
from jax.sharding import PartitionSpec as P

MESH = pl.DeviceIdType.MESH
NZ, NY, NX, WIN = 8, 8, 4, 4
FAR_FIRST = (4, 3, 5, 2, 6, 1, 7)
NEAR_FIRST = (1, 7, 2, 6, 3, 5, 4)


def kernel(ranks, owners, rhs, u, v, d, solved, updated, uall, vall, res, stage, sibb, comb, rsb, nag, xag,
           ux_s, ux_r, uy_s, uy_r, vy_s, vy_r, vx_s, vx_r, sib_s, sib_r, rs_s, rs_r, ag_s, ag_r, fw_s, fw_r):
    p, q = lax.axis_index("rows"), lax.axis_index("rhs")
    z, c, y, x = p // 2, p % 2, q // 4, q % 4

    def at_z(dz, core):
        return {"rows": lax.rem(z + dz, NZ) * 2 + core, "rhs": q}

    def at_y(dy):
        return {"rows": p, "rhs": lax.rem(y + dy, NY) * 4 + x}

    def at_x(dx):
        return {"rows": p, "rhs": y * 4 + lax.rem(x + dx, NX)}

    barrier = pltpu.get_barrier_semaphore()
    peers = [at_z(0, 1 - c)]
    peers += [at_z(dz, c) for dz in range(1, NZ)]
    peers += [at_y(1), at_y(NY - 1)] + [at_x(dx) for dx in range(1, NX)]
    for peer in peers:
        pl.semaphore_signal(barrier, inc=1, device_id=peer, device_id_type=MESH)
    pl.semaphore_wait(barrier, len(peers))

    sent = []

    def send(src, dst, s_sem, r_sem, peer):
        copy = pltpu.make_async_remote_copy(
            src_ref=src, dst_ref=dst, send_sem=s_sem, recv_sem=r_sem, device_id=peer, device_id_type=MESH
        )
        copy.start()
        sent.append(copy)

    def arrived(dst, s_sem, r_sem):
        pltpu.make_async_remote_copy(
            src_ref=dst, dst_ref=dst, send_sem=s_sem, recv_sem=r_sem, device_id=at_z(0, 1 - c), device_id_type=MESH
        ).wait_recv()

    def yy(dy):
        return lax.rem(y + dy + NY, NY)

    def gather_step(k, step):
        if step == 0:
            for dx in range(1, NX):
                send(u.at[0, k], uall.at[k, y, x], ux_s.at[k, dx], ux_r.at[k, dx], at_x(dx))
            uall[k, y, x] = u[0, k]
            vall[k, y, x] = v[0, k]
        if step == 1:
            for dx in range(1, NX):
                arrived(uall.at[k, y, lax.rem(x + NX - dx, NX)], ux_s.at[k, dx], ux_r.at[k, dx])
        if 1 <= step <= 4:
            h = step - 1
            if h > 0:
                arrived(uall.at[k, yy(-h)], uy_s.at[k, 0, h], uy_r.at[k, 0, h])
                arrived(uall.at[k, yy(h)], uy_s.at[k, 1, h], uy_r.at[k, 1, h])
            up, down = (uall.at[k, yy(-h)], uall.at[k, yy(h)])
            if h == 3:
                up, down = (up.at[pl.ds(0, 2)], down.at[pl.ds(2, 2)])
            send(up, up, uy_s.at[k, 0, h + 1], uy_r.at[k, 0, h + 1], at_y(1))
            send(down, down, uy_s.at[k, 1, h + 1], uy_r.at[k, 1, h + 1], at_y(NY - 1))
        if step == 5:
            arrived(uall.at[k, yy(4), pl.ds(0, 2)], uy_s.at[k, 0, 4], uy_r.at[k, 0, 4])
            arrived(uall.at[k, yy(4), pl.ds(2, 2)], uy_s.at[k, 1, 4], uy_r.at[k, 1, 4])
        if step <= 3:
            h = step
            if h > 0:
                arrived(vall.at[k, yy(-h), x], vy_s.at[k, 0, h], vy_r.at[k, 0, h])
                arrived(vall.at[k, yy(h), x], vy_s.at[k, 1, h], vy_r.at[k, 1, h])
            up, down = (vall.at[k, yy(-h), x], vall.at[k, yy(h), x])
            if h == 3:
                up, down = (up.at[pl.ds(0, 32)], down.at[pl.ds(32, 32)])
            send(up, up, vy_s.at[k, 0, h + 1], vy_r.at[k, 0, h + 1], at_y(1))
            send(down, down, vy_s.at[k, 1, h + 1], vy_r.at[k, 1, h + 1], at_y(NY - 1))
        if step == 4:
            arrived(vall.at[k, yy(4), x, pl.ds(0, 32)], vy_s.at[k, 0, 4], vy_r.at[k, 0, 4])
            arrived(vall.at[k, yy(4), x, pl.ds(32, 32)], vy_s.at[k, 1, 4], vy_r.at[k, 1, 4])
            for dx in range(1, NX):
                send(vall.at[k, :, x], vall.at[k, :, x], vx_s.at[k, dx], vx_r.at[k, dx], at_x(dx))
        if step == 5:
            for dx in range(1, NX):
                arrived(vall.at[k, :, lax.rem(x + NX - dx, NX)], vx_s.at[k, dx], vx_r.at[k, dx])

    todo = sorted(((2 * k + step, k, step) for k in range(WIN) for step in range(6)))
    done = set()

    def pump(count):
        for _ in range(min(count, len(todo))):
            _, k, step = todo.pop(0)
            gather_step(k, step)
            done.add((k, step))

    def pump_through(k):
        while (k, 5) not in done:
            pump(1)

    def gather_pieces(pieces, a):
        for dz in FAR_FIRST:
            send(pieces.at[p], pieces.at[p], ag_s.at[a, dz], ag_r.at[a, dz], at_z(dz, c))
        send(pieces.at[p], pieces.at[p], fw_s.at[a, 0], fw_r.at[a, 0], at_z(0, 1 - c))
        pump(2)
        for dz in NEAR_FIRST:
            piece = pieces.at[lax.rem(z + NZ - dz, NZ) * 2 + c]
            arrived(piece, ag_s.at[a, dz], ag_r.at[a, dz])
            send(piece, piece, fw_s.at[a, dz], fw_r.at[a, dz], at_z(0, 1 - c))
        for dz in range(NZ):
            piece = pieces.at[lax.rem(z + NZ - dz, NZ) * 2 + 1 - c]
            arrived(piece, fw_s.at[a, dz], fw_r.at[a, dz])

    stored = [owners[i] for i in range(16)]
    my_row = stored[0]
    for i in range(1, 16):
        my_row = jnp.where(p == i, stored[i], my_row)

    gather_step(0, 0)
    todo.pop(0)
    for g in range(NY):
        rows = rhs[0, pl.ds(256 * g, 256), :]
        stage[0, g] = rows.reshape(2, 128, 128)
        res[pl.ds(256 * g, 256), :] = rows.astype(jnp.float32)

    for j in range(WIN):
        mine = jnp.full((128, 128), my_row, jnp.int32) == j
        send(stage.at[j, :, 1 - c], sibb.at[j], sib_s.at[j], sib_r.at[j], at_z(0, 1 - c))
        pump(1)
        arrived(sibb.at[j], sib_s.at[j], sib_r.at[j])
        sib_row = stored[0]
        for i in range(1, 16):
            sib_row = jnp.where(p + 1 - 2 * c == i, stored[i], sib_row)
        sibs = jnp.full((128, 128), sib_row, jnp.int32) == j
        zero = jnp.zeros((128, 128), jnp.float32)
        for g in range(NZ):
            own = jnp.where(mine, stage[j, g, c].astype(jnp.float32), zero)
            other = jnp.where(sibs, sibb[j, g].astype(jnp.float32), own)
            comb[j, g] = other.astype(jnp.bfloat16)
        for dz in FAR_FIRST:
            send(comb.at[j, lax.rem(z + dz, NZ)], rsb.at[j, dz], rs_s.at[j, dz], rs_r.at[j, dz], at_z(dz, c))
        pump(1)
        total = comb[j, z].astype(jnp.float32)
        for dz in NEAR_FIRST:
            arrived(rsb.at[j, dz], rs_s.at[j, dz], rs_r.at[j, dz])
            total = total + rsb[j, dz].astype(jnp.float32)
        nag[j, p] = total.astype(jnp.bfloat16)
        gather_pieces(nag.at[j], 2 * j)
        acc = jnp.zeros((128, 128), jnp.float32)
        for g in range(NZ):
            acc += jnp.dot(
                d[j, :, pl.ds(256 * g, 256)], nag[j, pl.ds(2 * g, 2)].reshape(256, 128),
                preferred_element_type=jnp.float32,
            )
        solved[j] = acc.astype(jnp.bfloat16)
        xag[j, p] = acc.T.astype(jnp.bfloat16)
        gather_pieces(xag.at[j], 2 * j + 1)
        pump_through(j)
        ct = jnp.zeros((128, 256), jnp.float32)
        for g in range(NY):
            both = jnp.concatenate([xag[j, 2 * g], xag[j, 2 * g + 1]], axis=1)
            ct += jnp.dot(both, vall[j, g].reshape(256, 256), preferred_element_type=jnp.float32)
        keep = lax.broadcasted_iota(jnp.int32, (128, 256), 1) < jnp.where(j < my_row, ranks[0, j], 0)
        coeffs = jnp.where(keep, ct, 0.0).T.astype(jnp.bfloat16)
        for g in range(NY):
            rows = pl.ds(256 * g, 256)
            new = res[rows, :] - jnp.dot(
                uall[j, g].reshape(256, 256), coeffs, preferred_element_type=jnp.float32
            )
            if j < WIN - 1:
                res[rows, :] = new
                stage[j + 1, g] = new.astype(jnp.bfloat16).reshape(2, 128, 128)
            else:
                updated[0, rows, :] = new.astype(jnp.bfloat16)
    for copy in sent:
        copy.wait_send()


def body(rhs_blocks, left_u, left_v, tile_ranks, diag_inverse, row_owner):
    vmem, smem = (pl.BlockSpec(memory_space=pltpu.VMEM), pl.BlockSpec(memory_space=pltpu.SMEM))
    bf16 = jnp.bfloat16
    dma = pltpu.SemaphoreType.DMA
    return tuple(pl.pallas_call(
        kernel,
        out_shape=(
            jax.ShapeDtypeStruct((WIN, 128, 128), bf16),
            jax.ShapeDtypeStruct((1, 2048, 128), bf16),
        ),
        in_specs=[smem, smem, vmem, vmem, vmem, vmem],
        out_specs=(vmem, vmem),
        scratch_shapes=[
            pltpu.VMEM((WIN, NY, NX, 64, 256), bf16),
            pltpu.VMEM((WIN, NY, NX, 64, 256), bf16),
            pltpu.VMEM((2048, 128), jnp.float32),
            pltpu.VMEM((WIN, NZ, 2, 128, 128), bf16),
            pltpu.VMEM((WIN, NZ, 128, 128), bf16),
            pltpu.VMEM((WIN, NZ, 128, 128), bf16),
            pltpu.VMEM((WIN, NZ, 128, 128), bf16),
            pltpu.VMEM((WIN, 16, 128, 128), bf16),
            pltpu.VMEM((WIN, 16, 128, 128), bf16),
            dma((WIN, 4)), dma((WIN, 4)),
            dma((WIN, 2, 5)), dma((WIN, 2, 5)),
            dma((WIN, 2, 5)), dma((WIN, 2, 5)),
            dma((WIN, 4)), dma((WIN, 4)),
            dma((WIN,)), dma((WIN,)),
            dma((WIN, 8)), dma((WIN, 8)),
            dma((2 * WIN, 8)), dma((2 * WIN, 8)),
            dma((2 * WIN, 8)), dma((2 * WIN, 8)),
        ],
        compiler_params=pltpu.CompilerParams(
            collective_id=0, has_side_effects=True, vmem_limit_bytes=48 << 20
        ),
        name="substitution",
    )(tile_ranks, row_owner, rhs_blocks, left_u, left_v, diag_inverse))


def solution(mesh):
    return jax.shard_map(
        body,
        mesh=mesh,
        in_specs=(
            P("rows", None, "rhs"),
            P("rows", None, "rhs", None),
            P("rows", None, "rhs", None),
            P("rows", None),
            P(None, "rows", None),
            P(),
        ),
        out_specs=(P(None, "rows", "rhs"), P("rows", None, "rhs")),
        check_vma=False,
    )
```

time: 327 us -> 156 us (0.48)
  blocking collectives: 163 us -> 0 us
  Pallas kernels: 0 us -> 147 us
  waiting for transfers between devices: 98.1 us -> 0 us
  matrix products: 19.1 us -> 0 us
  between operations: 19.4 us -> 0.65 us
  starting transfers between devices: 13.9 us -> 0 us
  other arithmetic: 7.26 us -> 0 us
    pallas_call x0 -> x1, Pallas kernels: none -> 147 us  [body(): pl.pallas_call(kernel, out_shape=(jax.ShapeDtypeStruct((WIN, 128, 128), b...]
    all_to_all x4 -> x0, blocking collectives: 99.1 us -> none  [sent_and_summed(): lax.all_to_all(blocks, axis, split_axis=0, concat_axis=0, tiled=True)]
    all_gather x4 -> x0, blocking collectives: 63.6 us -> none  [body(): solution = lax.all_gather(solved_part, 'rows', axis=0, tiled=True)]
    all_to_all x4 -> x0, waiting for transfers between devices: 58.2 us -> none  [copy_for_each(): lax.all_to_all(jnp.broadcast_to(array[None], (peers, *array.shape)), axis...]
    all_gather x1 -> x0, waiting for transfers between devices: 39.9 us -> none  [sent_together(): filled, at, outs = (lax.all_gather(both, axis, axis=dim, tiled=True), 0, [])]
    dot_general x8 -> x0, matrix products: 19.1 us -> none  [the longest x4 16.7 us: right_product(): return jnp.dot(u_piece, coeffs, preferred_element_type=jnp.float32)]
    all_to_all x4 -> x0, starting transfers between devices: 13.9 us -> none  [copy_for_each(): lax.all_to_all(jnp.broadcast_to(array[None], (peers, *array.shape)), axis...]
    unnamed x3 -> x14, local copies, waits for them, and re-layouts: 0.78 us -> 7.19 us
  transfers between devices with their start and end apart: 5 -> 0, of which waited for: 5 -> 0; matrix products, arithmetic and copies ran while one was open for 3% -> 0% of each run, Pallas kernels for 0% -> 0%
where the time goes in v1:
time: 156 us; the launch traced here: 155 us
  Pallas kernels  147 us (94%)
  local copies, waits for them, and re-layouts  7.19 us (5%)
    pallas_call x1, Pallas kernels, body(): pl.pallas_call(kernel, out_shape=(jax.ShapeDtypeStruct((WIN, 128, 128), b...  147 us
    unnamed x14, local copies, waits for them, and re-layouts  7.19 us

profile of v1, /device:TPU:1, one launch (start us, length us, event | category | flops | bytes accessed | tf_op | source)
XLA Modules:
  0.0 155.3 jit_solution(16368134476386742082)
XLA Ops:
  0.6 0.0 copy-start
  0.6 1.6 %copy-done = bf16[4,128,2048]{2,1,0:T(8,128)(2,1)S(1)} copy-done((bf16[4,128,2048]{2,1,0:T(8,128)(2,1)S(1)}, bf16[4,128,2048]{2,1,0:T(8,128)(2,1)}, u32[]{:S(2)}) %copy-start) | copy-done | bytes 2097176
  2.2 0.0 copy-start.1
  2.2 1.0 copy-done.1
  3.3 0.0 copy-start.2
  3.3 0.9 copy-done.2
  4.2 0.0 copy-start.3
  4.2 0.9 copy-done.3
  5.1 0.0 copy-start.4
  5.1 0.7 copy-done.4
  5.7 0.0 copy-start.5
  5.7 0.7 copy-done.5
  6.4 147.4 %substitution.1 = (bf16[4,128,128]{2,1,0:T(8,128)(2,1)S(1)}, bf16[1,2048,128]{2,1,0:T(8,128)(2,1)S(1)}) custom-call(s32[1,4]{1,0:T(1,128)S(1)} %copy-done.4, s32[16]{0:T(128)S(1)} %copy-done.5, bf16[1,2048,128]{2,1,0:T(8,128)(2,1)S(1)} %copy-done.1, bf16[1,4,64,256]{3,2,1,0:T(8,128)(2,1)S(1)} %copy-done.2, bf16[1,4,64,256]{3,2,1,0:T(8,128)(2,1)S(1)} %copy-done.3, ...), custom_call_target="tpu_custom_call" | custom-call | tf_op jit(solution)/shard_map/substitution/pallas_call | solution.py:189
  153.8 0.7 copy.10
  154.5 0.8 copy.11
Async XLA Ops:
  0.6 1.6 %copy-start = (bf16[4,128,2048]{2,1,0:T(8,128)(2,1)S(1)}, bf16[4,128,2048]{2,1,0:T(8,128)(2,1)}, u32[]{:S(2)}) copy-start(bf16[4,128,2048]{2,1,0:T(8,128)(2,1)} %d.1) | copy-start | bytes 6291460
  2.2 1.0 copy-start.1
  3.3 0.9 copy-start.2
  4.2 0.9 copy-start.3
  5.1 0.7 copy-start.4
  5.7 0.7 copy-start.5

commit v2 on v0

v2 whole, which is shorter than its diff:
```python
import jax
import jax.numpy as jnp
from jax import lax
from jax.experimental import pallas as pl
from jax.experimental.pallas import tpu as pltpu
from jax.sharding import PartitionSpec as P

MESH = pl.DeviceIdType.MESH
NZ, NY, NX, WIN = 8, 8, 4, 4
NEAR = WIN - 1
FAR_FIRST = (4, 3, 5, 2, 6, 1, 7)
NEAR_FIRST = (1, 7, 2, 6, 3, 5, 4)
F32, BF16 = jnp.float32, jnp.bfloat16
BEGIN = {0: 0, 4: 2.5, 1: 5, 5: 6.5, 2: 9, 6: 10.5, 3: 12}


def dot(a, b):
    return jnp.dot(a, b, preferred_element_type=F32)


def kernel(ranks, owners, rhs, u, v, d, solved, updated, uall, vall, cu, cv, uown, vown, rin, dchip, res, stage,
           sibb, comb, rsb, nag, xag, cmine, cout, csib, ccomb, crs, cown, ysend, yrecv, lsem, ssem, rsem):
    p, q = lax.axis_index("rows"), lax.axis_index("rhs")
    z, c, y, x = p // 2, p % 2, q // 4, q % 4

    loads = []
    for i, (src, dst) in enumerate(
        ((u.at[0], uown), (v.at[0], vown), (rhs, rin), (d, dchip.at[:, pl.ds(0, 128)]))
    ):
        load = pltpu.make_async_copy(src, dst, lsem.at[i])
        load.start()
        loads.append(load)

    def at_z(dz, core):
        return {"rows": lax.rem(z + dz, NZ) * 2 + core, "rhs": q}

    def at_y(dy):
        return {"rows": p, "rhs": lax.rem(y + dy, NY) * 4 + x}

    def at_x(dx):
        return {"rows": p, "rhs": y * 4 + lax.rem(x + dx, NX)}

    sib = at_z(0, 1 - c)
    barrier = pltpu.get_barrier_semaphore()
    peers = [sib] + [at_z(dz, c) for dz in range(1, NZ)]
    peers += [at_y(1), at_y(NY - 1)] + [at_x(dx) for dx in range(1, NX)]
    for peer in peers:
        pl.semaphore_signal(barrier, inc=1, device_id=peer, device_id_type=MESH)

    numbers, sent = {}, []

    def copy_of(key, src, dst, peer):
        n = numbers.setdefault(key, len(numbers))
        return pltpu.make_async_remote_copy(
            src_ref=src, dst_ref=dst, send_sem=ssem.at[n], recv_sem=rsem.at[n], device_id=peer, device_id_type=MESH
        )

    def send(key, src, dst, peer):
        copy = copy_of(key, src, dst, peer)
        copy.start()
        sent.append(copy)

    def arrived(key, dst):
        copy_of(key, dst, dst, sib).wait_recv()

    def zz(dz):
        return lax.rem(z + NZ - dz, NZ)

    def yy(dy):
        return lax.rem(y + dy + NY, NY)

    def xx(dx):
        return lax.rem(x + NX - dx, NX)

    def gather_step(e, step):
        if e < WIN:
            ub, vb, ua, va = uown.at[e], vown.at[e], uall.at[e], vall.at[e]
        else:
            t = e - WIN
            ub, vb, ua, va = cown.at[0, t], cown.at[1, t], cu.at[t], cv.at[t]
        if step == 0:
            for dx in range(1, NX):
                send(("ux", e, dx), ub, ua.at[y, x], at_x(dx))
            ua[y, x] = ub[...]
            va[y, x] = vb[...]
        if step == 1:
            for dx in range(1, NX):
                arrived(("ux", e, dx), ua.at[y, xx(dx)])
        if 1 <= step <= 4:
            h = step - 1
            if h > 0:
                arrived(("uy+", e, h), ua.at[yy(-h)])
                arrived(("uy-", e, h), ua.at[yy(h)])
            up, down = (ua.at[yy(-h)], ua.at[yy(h)])
            if h == 3:
                up, down = (up.at[pl.ds(0, 2)], down.at[pl.ds(2, 2)])
            send(("uy+", e, h + 1), up, up, at_y(1))
            send(("uy-", e, h + 1), down, down, at_y(NY - 1))
        if step == 5:
            arrived(("uy+", e, 4), ua.at[yy(4), pl.ds(0, 2)])
            arrived(("uy-", e, 4), ua.at[yy(4), pl.ds(2, 2)])
        if step <= 3:
            h = step
            if h > 0:
                arrived(("vy+", e, h), va.at[yy(-h), x])
                arrived(("vy-", e, h), va.at[yy(h), x])
            up, down = (va.at[yy(-h), x], va.at[yy(h), x])
            if h == 3:
                up, down = (up.at[pl.ds(0, 32)], down.at[pl.ds(32, 32)])
            send(("vy+", e, h + 1), up, up, at_y(1))
            send(("vy-", e, h + 1), down, down, at_y(NY - 1))
        if step == 4:
            arrived(("vy+", e, 4), va.at[yy(4), x, pl.ds(0, 32)])
            arrived(("vy-", e, 4), va.at[yy(4), x, pl.ds(32, 32)])
            for dx in range(1, NX):
                send(("vx", e, dx), va.at[:, x], va.at[:, x], at_x(dx))
        if step == 5:
            for dx in range(1, NX):
                arrived(("vx", e, dx), va.at[:, xx(dx)])

    todo = sorted((b + step, e, step) for e, b in BEGIN.items() for step in range(6))
    done = set()

    def pump(count):
        for _ in range(min(count, len(todo))):
            _, e, step = todo.pop(0)
            gather_step(e, step)
            done.add((e, step))

    def pump_through(e):
        while (e, 5) not in done:
            pump(1)

    def ag_send(pieces, a):
        for dz in FAR_FIRST:
            send((a, dz), pieces.at[p], pieces.at[p], at_z(dz, c))
        send((a, "f", 0), pieces.at[p], pieces.at[p], sib)

    def ag_forward(pieces, a):
        for dz in NEAR_FIRST:
            piece = pieces.at[zz(dz) * 2 + c]
            arrived((a, dz), piece)
            send((a, "f", dz), piece, piece, sib)

    def ag_finish(pieces, a):
        for dz in range(NZ):
            arrived((a, "f", dz), pieces.at[zz(dz) * 2 + 1 - c])

    stored = [owners[i] for i in range(16)]
    my_row, sib_row = stored[0], stored[0]
    for i in range(1, 16):
        my_row = jnp.where(p == i, stored[i], my_row)
        sib_row = jnp.where(p + 1 - 2 * c == i, stored[i], sib_row)

    def is_row(row, j, shape):
        return jnp.full(shape, row, jnp.int32) == j

    def scatter(j, own, other):
        square = (128, 128)
        mine, sibs = is_row(my_row, j, square), is_row(sib_row, j, square)
        zero = jnp.zeros(square, F32)
        for g in range(NZ):
            far = jnp.where(sibs, other[g].astype(F32), zero)
            comb[j, g] = jnp.where(mine, own[g, c].astype(F32), far).astype(BF16)
        for dz in FAR_FIRST:
            send(("rs", j, dz), comb.at[j, lax.rem(z + dz, NZ)], rsb.at[j, dz], at_z(dz, c))

    def scattered(j):
        total = comb[j, z].astype(F32)
        for dz in NEAR_FIRST:
            arrived(("rs", j, dz), rsb.at[j, dz])
            total = total + rsb[j, dz].astype(F32)
        nag[j, p] = total.astype(BF16)
        ag_send(nag.at[j], ("n", j))

    def solve_far(j):
        acc = jnp.zeros((128, 128), F32)
        for g in range(NZ):
            acc += dot(dchip[j, pl.ds(0, 128), pl.ds(256 * g, 256)], nag[j, pl.ds(2 * g, 2)].reshape(256, 128))
        return acc

    def store_solved(j, value):
        solved[j] = value.astype(BF16)
        xag[j, p] = value.T.astype(BF16)
        ag_send(xag.at[j], ("x", j))

    def times_solved(j, factor):
        total = None
        for g in range(NY):
            both = jnp.concatenate([xag[j, 2 * g], xag[j, 2 * g + 1]], axis=1)
            term = dot(both, factor(g))
            total = term if total is None else total + term
        return total

    def near_term(t):
        coeffs = times_solved(t, lambda g: cv[t, g].reshape(256, 128)).T.astype(BF16)
        total = jnp.zeros((256, 128), F32)
        for g in range(NY):
            part = dot(cu[t, g].reshape(256, 128), coeffs).astype(BF16)
            total += dot(dchip[t + 1, :, pl.ds(256 * g, 256)], part)
        ysend[t] = total[128:]
        send(("y", t), ysend.at[t], yrecv.at[t], sib)
        return total[:128]

    def update(k):
        ct = times_solved(k, lambda g: vall[k, g].reshape(256, 256))
        keep = lax.broadcasted_iota(jnp.int32, (128, 256), 1) < jnp.where(k < my_row, ranks[0, k], 0)
        coeffs = jnp.where(keep, ct, 0.0).T.astype(BF16)
        for g in range(NY):
            old = rin[g].reshape(256, 128).astype(F32) if k == 0 else res[g]
            new = old - dot(uall[k, g].reshape(256, 256), coeffs)
            if k < WIN - 1:
                res[g] = new
            if k < WIN - 2:
                stage[k, g] = new.astype(BF16).reshape(2, 128, 128)
            if k == WIN - 1:
                updated[g] = new.astype(BF16).reshape(2, 128, 128)

    for load in loads[:3]:
        load.wait()
    for t in range(NEAR):
        half = (64, 128)
        mine = is_row(my_row, t + 1, half)
        left = is_row(c, 0, half)
        lane = lax.broadcasted_iota(jnp.int32, half, 1)
        for i, own in enumerate((uown, vown)):
            a, b = own[t, :, :128].astype(F32), own[t, :, 128:].astype(F32)
            a, b = jnp.where(mine, a, 0.0), jnp.where(mine, b, 0.0)
            if i == 1:
                a, b = jnp.where(lane < ranks[0, t], a, 0.0), jnp.where(lane + 128 < ranks[0, t], b, 0.0)
            cmine[i, t] = jnp.where(left, a, b)
            cout[i, t] = jnp.where(left, b, a).astype(BF16)

    pl.semaphore_wait(barrier, len(peers))
    send(("r", 0), rin.at[:, 1 - c], sibb.at[0], sib)
    send(("c",), cout, csib, sib)
    pump(1)
    arrived(("r", 0), sibb.at[0])
    scatter(0, rin, sibb.at[0])
    arrived(("c",), csib)
    for i in range(NZ):
        rows = pl.ds(16 * (i % 4), 16)
        ccomb[i] = (cmine[i // 4, :, rows] + csib[i // 4, :, rows].astype(F32)).astype(BF16)
    for dz in FAR_FIRST:
        send(("crs", dz), ccomb.at[lax.rem(z + dz, NZ)], crs.at[dz], at_z(dz, c))
    loads[3].wait()
    ownd = dchip.at[pl.ds(1, NEAR), pl.ds(0, 128)]
    send(("d",), ownd, dchip.at[pl.ds(1, NEAR), pl.ds(128, 128)], sib)
    pump(1)
    scattered(0)
    total = ccomb[z].astype(F32)
    for dz in NEAR_FIRST:
        arrived(("crs", dz), crs.at[dz])
        total = total + crs[dz].astype(F32)
    place = cown.at[z // 4, :, pl.ds(pl.multiple_of(16 * (z % 4), 16), 16)]
    place[...] = total.astype(BF16)
    for dz in FAR_FIRST:
        send(("cag", dz), place, place, at_z(dz, c))
    scatter(1, rin, sibb.at[0])
    pump(1)
    ag_forward(nag.at[0], ("n", 0))
    for dz in NEAR_FIRST:
        arrived(("cag", dz), cown.at[zz(dz) // 4, :, pl.ds(pl.multiple_of(16 * (zz(dz) % 4), 16), 16)])
    pump(1)
    ag_finish(nag.at[0], ("n", 0))
    store_solved(0, solve_far(0))
    pump(3)
    scattered(1)
    pump(3)
    arrived(("d",), dchip.at[pl.ds(1, NEAR), pl.ds(128, 128)])
    for j in range(WIN):
        ag_forward(xag.at[j], ("x", j))
        if j in (1, 2):
            scattered(j + 1)
        ag_finish(xag.at[j], ("x", j))
        if j < WIN - 1:
            pump_through(WIN + j)
            mine = near_term(j)
            ag_forward(nag.at[j + 1], ("n", j + 1))
            pump(1)
            ag_finish(nag.at[j + 1], ("n", j + 1))
            base = solve_far(j + 1) - mine
            arrived(("y", j), yrecv.at[j])
            store_solved(j + 1, base - yrecv[j])
        pump_through(j)
        update(j)
        if j < 2:
            send(("r", j + 1), stage.at[j, :, 1 - c], sibb.at[j + 1], sib)
            pump(2)
            arrived(("r", j + 1), sibb.at[j + 1])
            scatter(j + 2, stage.at[j], sibb.at[j + 1])
        pump(5)
    for copy in sent:
        copy.wait_send()


def body(rhs_blocks, left_u, left_v, tile_ranks, diag_inverse, row_owner):
    vmem, smem, hbm = (pl.BlockSpec(memory_space=s) for s in (pltpu.VMEM, pltpu.SMEM, pl.ANY))
    blocks = (NZ, 2, 128, 128)
    solved, updated = pl.pallas_call(
        kernel,
        out_shape=(jax.ShapeDtypeStruct((WIN, 128, 128), BF16), jax.ShapeDtypeStruct(blocks, BF16)),
        in_specs=[smem, smem, hbm, hbm, hbm, hbm],
        out_specs=(vmem, vmem),
        scratch_shapes=[
            pltpu.VMEM((WIN, NY, NX, 64, 256), BF16),
            pltpu.VMEM((WIN, NY, NX, 64, 256), BF16),
            pltpu.VMEM((NEAR, NY, NX, 64, 128), BF16),
            pltpu.VMEM((NEAR, NY, NX, 64, 128), BF16),
            pltpu.VMEM((WIN, 64, 256), BF16),
            pltpu.VMEM((WIN, 64, 256), BF16),
            pltpu.VMEM(blocks, BF16),
            pltpu.VMEM((WIN, 256, 2048), BF16),
            pltpu.VMEM((NZ, 256, 128), F32),
            pltpu.VMEM((2, *blocks), BF16),
            pltpu.VMEM((3, NZ, 128, 128), BF16),
            pltpu.VMEM((WIN, NZ, 128, 128), BF16),
            pltpu.VMEM((WIN, NZ, 128, 128), BF16),
            pltpu.VMEM((WIN, 16, 128, 128), BF16),
            pltpu.VMEM((WIN, 16, 128, 128), BF16),
            pltpu.VMEM((2, NEAR, 64, 128), F32),
            pltpu.VMEM((2, NEAR, 64, 128), BF16),
            pltpu.VMEM((2, NEAR, 64, 128), BF16),
            pltpu.VMEM((NZ, NEAR, 16, 128), BF16),
            pltpu.VMEM((NZ, NEAR, 16, 128), BF16),
            pltpu.VMEM((2, NEAR, 64, 128), BF16),
            pltpu.VMEM((NEAR, 128, 128), F32),
            pltpu.VMEM((NEAR, 128, 128), F32),
            pltpu.SemaphoreType.DMA((4,)),
            pltpu.SemaphoreType.DMA((400,)),
            pltpu.SemaphoreType.DMA((400,)),
        ],
        compiler_params=pltpu.CompilerParams(
            collective_id=0, has_side_effects=True, vmem_limit_bytes=48 << 20
        ),
        name="substitution",
    )(tile_ranks, row_owner, rhs_blocks.reshape(blocks), left_u, left_v, diag_inverse)
    return solved, updated.reshape(1, 2048, 128)


def solution(mesh):
    return jax.shard_map(
        body,
        mesh=mesh,
        in_specs=(
            P("rows", None, "rhs"),
            P("rows", None, "rhs", None),
            P("rows", None, "rhs", None),
            P("rows", None),
            P(None, "rows", None),
            P(),
        ),
        out_specs=(P(None, "rows", "rhs"), P("rows", None, "rhs")),
        check_vma=False,
    )
```

time: 327 us -> 172 us (0.53)
  Pallas kernels: 0 us -> 163 us
  blocking collectives: 163 us -> 0 us
  waiting for transfers between devices: 98.1 us -> 0 us
  matrix products: 19.1 us -> 0 us
  between operations: 19.4 us -> 0.65 us
  starting transfers between devices: 13.9 us -> 0 us
  other arithmetic: 7.26 us -> 0 us
    pallas_call x0 -> x1, Pallas kernels: none -> 163 us  [body(): pl.pallas_call(kernel, out_shape=(jax.ShapeDtypeStruct((WIN, 128, 128), B...]
    all_to_all x4 -> x0, blocking collectives: 99.1 us -> none  [sent_and_summed(): lax.all_to_all(blocks, axis, split_axis=0, concat_axis=0, tiled=True)]
    all_gather x4 -> x0, blocking collectives: 63.6 us -> none  [body(): solution = lax.all_gather(solved_part, 'rows', axis=0, tiled=True)]
    all_to_all x4 -> x0, waiting for transfers between devices: 58.2 us -> none  [copy_for_each(): lax.all_to_all(jnp.broadcast_to(array[None], (peers, *array.shape)), axis...]
    all_gather x1 -> x0, waiting for transfers between devices: 39.9 us -> none  [sent_together(): filled, at, outs = (lax.all_gather(both, axis, axis=dim, tiled=True), 0, [])]
    dot_general x8 -> x0, matrix products: 19.1 us -> none  [the longest x4 16.7 us: right_product(): return jnp.dot(u_piece, coeffs, preferred_element_type=jnp.float32)]
    all_to_all x4 -> x0, starting transfers between devices: 13.9 us -> none  [copy_for_each(): lax.all_to_all(jnp.broadcast_to(array[None], (peers, *array.shape)), axis...]
    unnamed x3 -> x14, local copies, waits for them, and re-layouts: 0.78 us -> 7.19 us
  transfers between devices with their start and end apart: 5 -> 0, of which waited for: 5 -> 0; matrix products, arithmetic and copies ran while one was open for 3% -> 0% of each run, Pallas kernels for 0% -> 0%
where the time goes in v2:
time: 172 us; the launch traced here: 171 us
  Pallas kernels  163 us (95%)
  local copies, waits for them, and re-layouts  7.19 us (4%)
    pallas_call x1, Pallas kernels, body(): pl.pallas_call(kernel, out_shape=(jax.ShapeDtypeStruct((WIN, 128, 128), B...  163 us
    unnamed x14, local copies, waits for them, and re-layouts  7.19 us

profile of v2, /device:TPU:1, one launch (start us, length us, event | category | flops | bytes accessed | tf_op | source)
XLA Modules:
  0.0 171.3 jit_solution(18335142034524699127)
XLA Ops:
  0.6 0.0 copy-start
  0.6 1.6 copy-done
  2.2 0.0 copy-start.1
  2.2 1.0 copy-done.1
  3.3 0.0 copy-start.2
  3.3 0.9 copy-done.2
  4.2 0.0 copy-start.3
  4.2 0.9 copy-done.3
  5.1 0.0 copy-start.4
  5.1 0.7 copy-done.4
  5.7 0.0 copy-start.5
  5.7 0.7 copy-done.5
  6.4 163.4 %substitution.1 = (bf16[4,128,128]{2,1,0:T(8,128)(2,1)S(1)}, bf16[8,2,128,128]{3,2,1,0:T(8,128)(2,1)S(1)}) custom-call(s32[1,4]{1,0:T(1,128)S(1)} %copy-done.4, s32[16]{0:T(128)S(1)} %copy-done.5, bf16[8,2,128,128]{3,2,1,0:T(8,128)(2,1)S(1)} %bitcast.3, bf16[1,4,64,256]{3,2,1,0:T(8,128)(2,1)S(1)} %copy-done.2, bf16[1,4,64,256]{3,2,1,0:T(8,128)(2,1)S(1)} %copy-done.3, ...), custom_call_target="tpu_custom_call" | custom-call | tf_op jit(solution)/shard_map/substitution/pallas_call | solution.py:300
  169.8 0.7 copy.10
  170.5 0.8 copy.11
Async XLA Ops:
  0.6 1.6 copy-start
  2.2 1.0 copy-start.1
  3.3 0.9 copy-start.2
  4.2 0.9 copy-start.3
  5.1 0.7 copy-start.4
  5.7 0.7 copy-start.5

commit v3 on v2

v3 whole, which is shorter than its diff:
```python
import jax
import jax.numpy as jnp
from jax import lax
from jax.experimental import pallas as pl
from jax.experimental.pallas import tpu as pltpu
from jax.sharding import PartitionSpec as P

MESH = pl.DeviceIdType.MESH
NZ, NY, NX, WIN = 8, 8, 4, 4
FAR_FIRST = (4, 3, 5, 2, 6, 1, 7)
NEAR_FIRST = (1, 7, 2, 6, 3, 5, 4)
PAIRS = ((1, 0), (3, 2))
F32, BF16 = jnp.float32, jnp.bfloat16
OWN = {"m0": (0, 2), "m2": (2, 2)}
ORDER = (
    "m0v0", "m0u0", "m0v1", "m0u1", "m0v2", "m0v3", "m0u2", "p1_0", "m0v4", "p1_1", "m0u3", "p1_2", "m0u4", "p1_3",
    "m0u5", "m0v5", "m0v6", "m0u6", "m2v0", "m2u0", "m2v1", "m2u1", "m2v2", "m2v3", "m2u2", "p3_0", "m2v4", "m2u3",
    "p3_1", "m2u4", "p3_2", "m2v5", "p3_3", "m2u5", "m2v6", "m2u6",
)


def dot(a, b):
    return jnp.dot(a, b, preferred_element_type=F32)


def kernel(ranks, owners, rhs, u, v, d, solved, updated, uall, vall, cuv, uown, vown, rin, dchip, res,
           stage, sibb, comb, rsb, nag, xag, cout, crs, cown, ysend, yrecv, lsem, ssem, rsem):
    p, q = lax.axis_index("rows"), lax.axis_index("rhs")
    z, c, y, x = p // 2, p % 2, q // 4, q % 4

    loads = []
    for i, (src, dst) in enumerate(
        ((u.at[0], uown), (v.at[0], vown), (rhs, rin), (d, dchip.at[:, pl.ds(0, 128)]))
    ):
        load = pltpu.make_async_copy(src, dst, lsem.at[i])
        load.start()
        loads.append(load)

    def at_z(dz, core):
        return {"rows": lax.rem(z + dz, NZ) * 2 + core, "rhs": q}

    def at_y(dy):
        return {"rows": p, "rhs": lax.rem(y + dy, NY) * 4 + x}

    def at_x(dx):
        return {"rows": p, "rhs": y * 4 + lax.rem(x + dx, NX)}

    sib = at_z(0, 1 - c)
    ring = [(dz, core) for dz in FAR_FIRST for core in (c, 1 - c)] + [(0, 1 - c)]
    barrier = pltpu.get_barrier_semaphore()
    peers = [at_z(dz, core) for dz, core in ring]
    peers += [at_y(dy) for dy in range(1, NY)] + [at_x(dx) for dx in range(1, NX)]
    for peer in peers:
        pl.semaphore_signal(barrier, inc=1, device_id=peer, device_id_type=MESH)

    numbers, sent = {}, []

    def copy_of(key, src, dst, peer):
        n = numbers.setdefault(key, len(numbers))
        return pltpu.make_async_remote_copy(
            src_ref=src, dst_ref=dst, send_sem=ssem.at[n], recv_sem=rsem.at[n], device_id=peer, device_id_type=MESH
        )

    def send(key, src, dst, peer):
        copy = copy_of(key, src, dst, peer)
        copy.start()
        sent.append(copy)

    def arrived(key, dst):
        copy_of(key, dst, dst, sib).wait_recv()

    def zz(dz):
        return lax.rem(z + NZ - dz, NZ)

    def yy(dy):
        return lax.rem(y + dy + NY, NY)

    def xx(dx):
        return lax.rem(x + NX - dx, NX)

    def place_own(own, into):
        for i in range(own.shape[0]):
            into[i, y, x] = own[i]

    def y_first(key, own, into, step):
        if step == 0:
            place_own(own, into)
        if 1 <= step <= 4:
            arrive = [into.at[:, yy(-step), x], into.at[:, yy(step), x]]
            if step == 4:
                arrive = [arrive[0].at[:, pl.ds(0, 32)], arrive[1].at[:, pl.ds(32, 32)]]
            arrived((key, "y+", step), arrive[0])
            arrived((key, "y-", step), arrive[1])
        if step <= 3:
            up, down = (into.at[:, yy(-step), x], into.at[:, yy(step), x])
            if step == 3:
                up, down = (up.at[:, pl.ds(0, 32)], down.at[:, pl.ds(32, 32)])
            send((key, "y+", step + 1), up, up, at_y(1))
            send((key, "y-", step + 1), down, down, at_y(NY - 1))
        if step == 4:
            send((key, "x+", 1), into.at[:, :, x], into.at[:, :, x], at_x(1))
            send((key, "x-", 1), into.at[:, :, x], into.at[:, :, x], at_x(NX - 1))
        low, high = pl.ds(0, 4), pl.ds(4, 4)
        if step == 5:
            arrived((key, "x+", 1), into.at[:, :, xx(1)])
            arrived((key, "x-", 1), into.at[:, :, xx(-1)])
            send((key, "x+", 2), into.at[:, low, xx(1)], into.at[:, low, xx(1)], at_x(1))
            send((key, "x-", 2), into.at[:, high, xx(-1)], into.at[:, high, xx(-1)], at_x(NX - 1))
        if step == 6:
            arrived((key, "x+", 2), into.at[:, low, xx(2)])
            arrived((key, "x-", 2), into.at[:, high, xx(2)])

    def x_first(key, own, into, step):
        if step == 0:
            for dx in range(1, NX):
                send((key, "x", dx), own, into.at[:, y, x], at_x(dx))
            place_own(own, into)
        if step == 1:
            for dx in range(1, NX):
                arrived((key, "x", dx), into.at[:, y, xx(dx)])
        h = step - 1
        if 1 <= h <= 4:
            arrive = [into.at[:, yy(-h)], into.at[:, yy(h)]]
            if h == 4:
                arrive = [arrive[0].at[:, pl.ds(0, 2)], arrive[1].at[:, pl.ds(2, 2)]]
            arrived((key, "y+", h), arrive[0])
            arrived((key, "y-", h), arrive[1])
        if 0 <= h <= 3:
            up, down = (into.at[:, yy(-h)], into.at[:, yy(h)])
            if h == 3:
                up, down = (up.at[:, pl.ds(0, 2)], down.at[:, pl.ds(2, 2)])
            send((key, "y+", h + 1), up, up, at_y(1))
            send((key, "y-", h + 1), down, down, at_y(NY - 1))

    def pair_step(t, step):
        into, low, high = cuv.at[:, t], pl.ds(0, 4), pl.ds(4, 4)
        if step == 0:
            for dy in FAR_FIRST:
                send(("py", t, dy), cown.at[:, t], into.at[:, y, x], at_y(dy))
            for i in range(2):
                cuv[i, t, y, x] = cown[i, t]
        if step == 1:
            for dy in NEAR_FIRST:
                arrived(("py", t, dy), into.at[:, yy(-dy), x])
            send(("px+", t, 1), into.at[:, :, x], into.at[:, :, x], at_x(1))
            send(("px-", t, 1), into.at[:, :, x], into.at[:, :, x], at_x(NX - 1))
        if step == 2:
            arrived(("px+", t, 1), into.at[:, :, xx(1)])
            arrived(("px-", t, 1), into.at[:, :, xx(-1)])
            send(("px+", t, 2), into.at[:, low, xx(1)], into.at[:, low, xx(1)], at_x(1))
            send(("px-", t, 2), into.at[:, high, xx(-1)], into.at[:, high, xx(-1)], at_x(NX - 1))
        if step == 3:
            arrived(("px+", t, 2), into.at[:, low, xx(2)])
            arrived(("px-", t, 2), into.at[:, high, xx(2)])

    def take(name, part, step):
        if name == "p1" or name == "p3":
            pair_step(int(name[1]) // 2, step)
        else:
            i, first = (0, x_first) if part == "u" else (1, y_first)
            group = pl.ds(*OWN[name])
            first((name, part), (uown, vown)[i].at[group], (uall, vall)[i].at[group], step)

    todo = list(ORDER)
    done = set()

    def pump(count):
        for _ in range(min(count, len(todo))):
            item = todo.pop(0)
            take(item[:2], item[2], int(item[3]))
            done.add(item)

    def pump_through(name):
        last = {name + "_3"} if name[0] == "p" else {name + "u6", name + "v6"}
        while not last <= done:
            pump(1)

    def ag_send(pieces, a):
        for dz in FAR_FIRST:
            send((a, dz), pieces.at[p], pieces.at[p], at_z(dz, c))
        send((a, "f", 0), pieces.at[p], pieces.at[p], sib)

    def ag_forward(pieces, a):
        for dz in NEAR_FIRST:
            piece = pieces.at[zz(dz) * 2 + c]
            arrived((a, dz), piece)
            send((a, "f", dz), piece, piece, sib)

    def ag_finish(pieces, a):
        for dz in range(NZ):
            arrived((a, "f", dz), pieces.at[zz(dz) * 2 + 1 - c])

    stored = [owners[i] for i in range(16)]
    my_row, sib_row = stored[0], stored[0]
    holder = [jnp.int32(0) for _ in range(WIN)]
    for i in range(16):
        my_row = jnp.where(p == i, stored[i], my_row)
        sib_row = jnp.where(p + 1 - 2 * c == i, stored[i], sib_row)
        holder = [jnp.where(stored[i] == j, i, h) for j, h in enumerate(holder)]

    def scatter(j, own, other):
        square = (128, 128)
        mine = jnp.full(square, my_row, jnp.int32) == j
        sibs = jnp.full(square, sib_row, jnp.int32) == j
        for g in range(NZ):
            far = jnp.where(sibs, other[g].astype(F32), 0.0)
            comb[j, g] = jnp.where(mine, own[g, c].astype(F32), far).astype(BF16)
        for dz in FAR_FIRST:
            send(("rs", j, dz), comb.at[j, lax.rem(z + dz, NZ)], rsb.at[j, dz], at_z(dz, c))

    def scattered(j):
        total = comb[j, z].astype(F32)
        for dz in NEAR_FIRST:
            arrived(("rs", j, dz), rsb.at[j, dz])
            total = total + rsb[j, dz].astype(F32)
        nag[j, p] = total.astype(BF16)

    def solve_far(j):
        acc = jnp.zeros((128, 128), F32)
        for g in range(NZ):
            acc += dot(dchip[j, pl.ds(0, 128), pl.ds(256 * g, 256)], nag[j, pl.ds(2 * g, 2)].reshape(256, 128))
        return acc

    def store_solved(j, value):
        solved[j] = value.astype(BF16)
        xag[j, p] = value.T.astype(BF16)
        ag_send(xag.at[j], ("x", j))

    def times_solved(j, factor):
        total = None
        for g in range(NY):
            both = jnp.concatenate([xag[j, 2 * g], xag[j, 2 * g + 1]], axis=1)
            term = dot(both, factor(g))
            total = term if total is None else total + term
        return total

    def pair_term(j, k):
        t = PAIRS.index((j, k))
        coeffs = times_solved(k, lambda g: cuv[1, t, g].reshape(256, 128)).T.astype(BF16)
        total = jnp.zeros((256, 128), F32)
        for g in range(NY):
            part = dot(cuv[0, t, g].reshape(256, 128), coeffs).astype(BF16)
            total += dot(dchip[j, :, pl.ds(256 * g, 256)], part)
        return total

    def update(k):
        ct = times_solved(k, lambda g: vall[k, g].reshape(256, 256))
        keep = lax.broadcasted_iota(jnp.int32, (128, 256), 1) < jnp.where(k < my_row, ranks[0, k], 0)
        coeffs = jnp.where(keep, ct, 0.0).T.astype(BF16)
        for g in range(NY):
            old = rin[g].reshape(256, 128).astype(F32) if k == 0 else res[g]
            new = old - dot(uall[k, g].reshape(256, 256), coeffs)
            if k < WIN - 1:
                res[g] = new
            if k == 1:
                stage[g] = new.astype(BF16).reshape(2, 128, 128)
            if k == WIN - 1:
                updated[g] = new.astype(BF16).reshape(2, 128, 128)

    for load in loads[:3]:
        load.wait()
    lane = lax.broadcasted_iota(jnp.int32, (64, 128), 1)
    for t, (_, k) in enumerate(PAIRS):
        for core in range(2):
            lanes = pl.ds(128 * core, 128)
            us = uown[k, :, lanes].reshape(4, 16, 128)
            vs = vown[k, :, lanes].astype(F32)
            vs = jnp.where(lane + 128 * core < ranks[0, k], vs, 0.0).astype(BF16).reshape(4, 16, 128)
            for i in range(4):
                cout[2 * i + core, t] = us[i]
                cout[8 + 2 * i + core, t] = vs[i]

    pl.semaphore_wait(barrier, len(peers))
    send(("r", 0), rin.at[:, 1 - c], sibb.at[0], sib)
    for i, (dz, core) in enumerate(ring):
        to = lax.rem(z + dz, NZ) * 2 + core
        send(("c", i), cout.at[to], crs.at[p], at_z(dz, core))
    pump(2)
    crs[p] = cout[p]
    arrived(("r", 0), sibb.at[0])
    scatter(0, rin, sibb.at[0])
    scatter(1, rin, sibb.at[0])
    loads[3].wait()
    near_d = [dchip.at[j, pl.ds(0, 128)] for j, _ in PAIRS]
    far_d = [dchip.at[j, pl.ds(128, 128)] for j, _ in PAIRS]
    for t in range(len(PAIRS)):
        send(("d", t), near_d[t], far_d[t], sib)
    pump(2)
    for i, (dz, core) in enumerate(ring):
        arrived(("c", i), crs.at[zz(dz) * 2 + core])
    part = pl.ds(pl.multiple_of(16 * (z % 4), 16), 16)
    for t, (j, _) in enumerate(PAIRS):
        cown[z // 4, t, part] = crs[holder[j], t]
    for dz in FAR_FIRST:
        place = cown.at[z // 4, :, part]
        send(("cag", dz), place, place, at_z(dz, c))
    pump(1)
    scattered(0)
    ag_send(nag.at[0], "n0")
    pump(2)
    for dz in NEAR_FIRST:
        arrived(("cag", dz), cown.at[zz(dz) // 4, :, pl.ds(pl.multiple_of(16 * (zz(dz) % 4), 16), 16)])
    pump(2)
    scattered(1)
    ag_forward(nag.at[0], "n0")
    ag_finish(nag.at[0], "n0")
    for j in range(WIN):
        even = j % 2 == 0
        if even:
            store_solved(j, solve_far(j))
            ag_send(nag.at[j + 1], "n" + str(j + 1))
        pump((2, 4, 4, 0)[j])
        ag_forward(xag.at[j], ("x", j))
        pump((1, 0, 0, 0)[j])
        ag_finish(xag.at[j], ("x", j))
        if even:
            t = j // 2
            pump_through("p" + str(j + 1))
            arrived(("d", t), far_d[t])
            term = pair_term(j + 1, j)
            ysend[t] = term[128:]
            send(("y", t), ysend.at[t], yrecv.at[t], sib)
            ag_forward(nag.at[j + 1], "n" + str(j + 1))
            ag_finish(nag.at[j + 1], "n" + str(j + 1))
            known = solve_far(j + 1) - term[:128]
            arrived(("y", t), yrecv.at[t])
            store_solved(j + 1, known - yrecv[t])
            pump_through("m" + str(j))
        update(j)
        if j == 1:
            send(("r", 1), stage.at[:, 1 - c], sibb.at[1], sib)
            arrived(("r", 1), sibb.at[1])
            scatter(2, stage, sibb.at[1])
            scatter(3, stage, sibb.at[1])
            pump(3)
            scattered(2)
            ag_send(nag.at[2], "n2")
            pump(3)
            scattered(3)
            ag_forward(nag.at[2], "n2")
            ag_finish(nag.at[2], "n2")
    for copy in sent:
        copy.wait_send()


def body(rhs_blocks, left_u, left_v, tile_ranks, diag_inverse, row_owner):
    vmem, smem, hbm = (pl.BlockSpec(memory_space=s) for s in (pltpu.VMEM, pltpu.SMEM, pl.ANY))
    blocks = (NZ, 2, 128, 128)
    pairs = len(PAIRS)
    solved, updated = pl.pallas_call(
        kernel,
        out_shape=(jax.ShapeDtypeStruct((WIN, 128, 128), BF16), jax.ShapeDtypeStruct(blocks, BF16)),
        in_specs=[smem, smem, hbm, hbm, hbm, hbm],
        out_specs=(vmem, vmem),
        scratch_shapes=[
            pltpu.VMEM((WIN, NY, NX, 64, 256), BF16),
            pltpu.VMEM((WIN, NY, NX, 64, 256), BF16),
            pltpu.VMEM((2, pairs, NY, NX, 64, 128), BF16),
            pltpu.VMEM((WIN, 64, 256), BF16),
            pltpu.VMEM((WIN, 64, 256), BF16),
            pltpu.VMEM(blocks, BF16),
            pltpu.VMEM((WIN, 256, 2048), BF16),
            pltpu.VMEM((NZ, 256, 128), F32),
            pltpu.VMEM(blocks, BF16),
            pltpu.VMEM((2, NZ, 128, 128), BF16),
            pltpu.VMEM((WIN, NZ, 128, 128), BF16),
            pltpu.VMEM((WIN, NZ, 128, 128), BF16),
            pltpu.VMEM((WIN, 16, 128, 128), BF16),
            pltpu.VMEM((WIN, 16, 128, 128), BF16),
            pltpu.VMEM((16, pairs, 16, 128), BF16),
            pltpu.VMEM((16, pairs, 16, 128), BF16),
            pltpu.VMEM((2, pairs, 64, 128), BF16),
            pltpu.VMEM((pairs, 128, 128), F32),
            pltpu.VMEM((pairs, 128, 128), F32),
            pltpu.SemaphoreType.DMA((4,)),
            pltpu.SemaphoreType.DMA((400,)),
            pltpu.SemaphoreType.DMA((400,)),
        ],
        compiler_params=pltpu.CompilerParams(
            collective_id=0, has_side_effects=True, vmem_limit_bytes=62 << 20
        ),
        name="substitution",
    )(tile_ranks, row_owner, rhs_blocks.reshape(blocks), left_u, left_v, diag_inverse)
    return solved, updated.reshape(1, 2048, 128)


def solution(mesh):
    return jax.shard_map(
        body,
        mesh=mesh,
        in_specs=(
            P("rows", None, "rhs"),
            P("rows", None, "rhs", None),
            P("rows", None, "rhs", None),
            P("rows", None),
            P(None, "rows", None),
            P(),
        ),
        out_specs=(P(None, "rows", "rhs"), P("rows", None, "rhs")),
        check_vma=False,
    )
```

time: 172 us -> 140 us (0.81)
  Pallas kernels: 163 us -> 136 us
  local copies, waits for them, and re-layouts: 7.19 us -> 3.44 us
    pallas_call x1, Pallas kernels: 163 us -> 136 us  [body(): pl.pallas_call(kernel, out_shape=(jax.ShapeDtypeStruct((WIN, 128, 128), B...]
    unnamed x14 -> x2, local copies, waits for them, and re-layouts: 7.19 us -> 3.44 us
where the time goes in v3:
time: 140 us
  Pallas kernels  136 us (97%)
  local copies, waits for them, and re-layouts  3.44 us (2%)
    pallas_call x1, Pallas kernels, body(): pl.pallas_call(kernel, out_shape=(jax.ShapeDtypeStruct((WIN, 128, 128), B...  136 us
    unnamed x2, local copies, waits for them, and re-layouts  3.44 us

profile of v3, /device:TPU:1, one launch (start us, length us, event | category | flops | bytes accessed | tf_op | source)
XLA Modules:
  0.0 139.7 jit_solution(10461931583851341717)
XLA Ops:
  0.6 135.7 %substitution.1 = (bf16[4,128,128]{2,1,0:T(8,128)(2,1)}, bf16[8,2,128,128]{3,2,1,0:T(8,128)(2,1)}) custom-call(s32[1,4]{1,0:T(1,128)} %ranks.1, s32[16]{0:T(128)} %owners.1, bf16[8,2,128,128]{3,2,1,0:T(8,128)(2,1)} %bitcast.3, bf16[1,4,64,256]{3,2,1,0:T(8,128)(2,1)} %u.1, bf16[1,4,64,256]{3,2,1,0:T(8,128)(2,1)} %v.1, bf16[4,128,2048]{2,1,0:T(8,128)(2,1)} %d.1), custom_call_target="tpu_custom_call" | custom-call | tf_op jit(solution)/shard_map/substitution/pallas_call | solution.py:350
  136.3 1.6 %copy.10 = bf16[4,128,128]{2,1,0:T(8,128)(2,1)} copy(bf16[4,128,128]{2,1,0:T(8,128)(2,1)} %get-tuple-element.8) | data formatting | bytes 262144
  137.9 1.9 %copy.11 = bf16[1,2048,128]{2,1,0:T(8,128)(2,1)} copy(bf16[1,2048,128]{2,1,0:T(8,128)(2,1)} %bitcast.2) | data formatting | bytes 1048576

commit v4 on v3

--- a/solution.py
+++ b/solution.py
@@ -13,9 +13,9 @@
 F32, BF16 = jnp.float32, jnp.bfloat16
 OWN = {"m0": (0, 2), "m2": (2, 2)}
 ORDER = (
-    "m0v0", "m0u0", "m0v1", "m0u1", "m0v2", "m0v3", "m0u2", "p1_0", "m0v4", "p1_1", "m0u3", "p1_2", "m0u4", "p1_3",
-    "m0u5", "m0v5", "m0v6", "m0u6", "m2v0", "m2u0", "m2v1", "m2u1", "m2v2", "m2v3", "m2u2", "p3_0", "m2v4", "m2u3",
-    "p3_1", "m2u4", "p3_2", "m2v5", "p3_3", "m2u5", "m2v6", "m2u6",
+    "m0v0", "m0u0", "m0v1", "m0u1", "m0v2", "m0v3", "m0u2", "p1_0", "m0v4", "p1_1", "m0u3", "p1_2", "m0v5", "m0u4",
+    "p1_3", "m0v6", "m0u5", "m0u6", "m2v0", "m2u0", "m2v1", "m2u1", "m2v2", "m2v3", "m2u2", "p3_0", "m2v4", "m2u3",
+    "p3_1", "m2v5", "m2u4", "p3_2", "m2v6", "p3_3", "m2u5", "m2u6",
 )
 
 
@@ -279,7 +279,6 @@
     crs[p] = cout[p]
     arrived(("r", 0), sibb.at[0])
     scatter(0, rin, sibb.at[0])
-    scatter(1, rin, sibb.at[0])
     loads[3].wait()
     near_d = [dchip.at[j, pl.ds(0, 128)] for j, _ in PAIRS]
     far_d = [dchip.at[j, pl.ds(128, 128)] for j, _ in PAIRS]
@@ -297,17 +296,19 @@
     pump(1)
     scattered(0)
     ag_send(nag.at[0], "n0")
+    scatter(1, rin, sibb.at[0])
     pump(2)
     for dz in NEAR_FIRST:
         arrived(("cag", dz), cown.at[zz(dz) // 4, :, pl.ds(pl.multiple_of(16 * (zz(dz) % 4), 16), 16)])
     pump(2)
-    scattered(1)
     ag_forward(nag.at[0], "n0")
     ag_finish(nag.at[0], "n0")
     for j in range(WIN):
         even = j % 2 == 0
         if even:
             store_solved(j, solve_far(j))
+            pump(1)
+            scattered(j + 1)
             ag_send(nag.at[j + 1], "n" + str(j + 1))
         pump((2, 4, 4, 0)[j])
         ag_forward(xag.at[j], ("x", j))
@@ -331,12 +332,11 @@
             send(("r", 1), stage.at[:, 1 - c], sibb.at[1], sib)
             arrived(("r", 1), sibb.at[1])
             scatter(2, stage, sibb.at[1])
-            scatter(3, stage, sibb.at[1])
             pump(3)
             scattered(2)
             ag_send(nag.at[2], "n2")
+            scatter(3, stage, sibb.at[1])
             pump(3)
-            scattered(3)
             ag_forward(nag.at[2], "n2")
             ag_finish(nag.at[2], "n2")
     for copy in sent:

time: 140 us -> 133 us (0.950)
  Pallas kernels: 136 us -> 129 us
    pallas_call x1, Pallas kernels: 136 us -> 129 us  [body(): pl.pallas_call(kernel, out_shape=(jax.ShapeDtypeStruct((WIN, 128, 128), B...]
where the time goes in v4:
time: 133 us
  Pallas kernels  129 us (97%)
  local copies, waits for them, and re-layouts  3.44 us (3%)
    pallas_call x1, Pallas kernels, body(): pl.pallas_call(kernel, out_shape=(jax.ShapeDtypeStruct((WIN, 128, 128), B...  129 us
    unnamed x2, local copies, waits for them, and re-layouts  3.44 us

profile of v4, /device:TPU:1, one launch (start us, length us, event | category | flops | bytes accessed | tf_op | source)
XLA Modules:
  0.0 133.0 jit_solution(2638081386666988944)
XLA Ops:
  0.6 128.9 %substitution.1 = (bf16[4,128,128]{2,1,0:T(8,128)(2,1)}, bf16[8,2,128,128]{3,2,1,0:T(8,128)(2,1)}) custom-call(s32[1,4]{1,0:T(1,128)} %ranks.1, s32[16]{0:T(128)} %owners.1, bf16[8,2,128,128]{3,2,1,0:T(8,128)(2,1)} %bitcast.3, bf16[1,4,64,256]{3,2,1,0:T(8,128)(2,1)} %u.1, bf16[1,4,64,256]{3,2,1,0:T(8,128)(2,1)} %v.1, bf16[4,128,2048]{2,1,0:T(8,128)(2,1)} %d.1), custom_call_target="tpu_custom_call" | custom-call | tf_op jit(solution)/shard_map/substitution/pallas_call | solution.py:350
  129.5 1.6 %copy.10 = bf16[4,128,128]{2,1,0:T(8,128)(2,1)} copy(bf16[4,128,128]{2,1,0:T(8,128)(2,1)} %get-tuple-element.8) | data formatting | bytes 262144
  131.1 1.9 %copy.11 = bf16[1,2048,128]{2,1,0:T(8,128)(2,1)} copy(bf16[1,2048,128]{2,1,0:T(8,128)(2,1)} %bitcast.2) | data formatting | bytes 1048576

commit v5 on v4

--- a/solution.py
+++ b/solution.py
@@ -14,8 +14,8 @@
 OWN = {"m0": (0, 2), "m2": (2, 2)}
 ORDER = (
     "m0v0", "m0u0", "m0v1", "m0u1", "m0v2", "m0v3", "m0u2", "p1_0", "m0v4", "p1_1", "m0u3", "p1_2", "m0v5", "m0u4",
-    "p1_3", "m0v6", "m0u5", "m0u6", "m2v0", "m2u0", "m2v1", "m2u1", "m2v2", "m2v3", "m2u2", "p3_0", "m2v4", "m2u3",
-    "p3_1", "m2v5", "m2u4", "p3_2", "m2v6", "p3_3", "m2u5", "m2u6",
+    "p1_3", "m0v6", "m0u5", "m0u6", "m2v0", "m2u0", "m2v1", "m2u1", "m2v2", "m2v3", "p3_0", "m2u2", "m2v4", "p3_1",
+    "m2u3", "p3_2", "m2v5", "m2u4", "p3_3", "m2v6", "m2u5", "m2u6",
 )
 
 

time: 133 us -> 133 us (level)
  no operation moved by 1% of the time
where the time goes in v5:
time: 133 us
  Pallas kernels  129 us (97%)
  local copies, waits for them, and re-layouts  3.44 us (3%)
    pallas_call x1, Pallas kernels, body(): pl.pallas_call(kernel, out_shape=(jax.ShapeDtypeStruct((WIN, 128, 128), B...  129 us
    unnamed x2, local copies, waits for them, and re-layouts  3.44 us

profile of v5, /device:TPU:1, one launch (start us, length us, event | category | flops | bytes accessed | tf_op | source)
XLA Modules:
  0.0 132.6 jit_solution(17132241916930889708)
XLA Ops:
  0.6 128.6 %substitution.1 = (bf16[4,128,128]{2,1,0:T(8,128)(2,1)}, bf16[8,2,128,128]{3,2,1,0:T(8,128)(2,1)}) custom-call(s32[1,4]{1,0:T(1,128)} %ranks.1, s32[16]{0:T(128)} %owners.1, bf16[8,2,128,128]{3,2,1,0:T(8,128)(2,1)} %bitcast.3, bf16[1,4,64,256]{3,2,1,0:T(8,128)(2,1)} %u.1, bf16[1,4,64,256]{3,2,1,0:T(8,128)(2,1)} %v.1, bf16[4,128,2048]{2,1,0:T(8,128)(2,1)} %d.1), custom_call_target="tpu_custom_call" | custom-call | tf_op jit(solution)/shard_map/substitution/pallas_call | solution.py:350
  129.2 1.6 %copy.10 = bf16[4,128,128]{2,1,0:T(8,128)(2,1)} copy(bf16[4,128,128]{2,1,0:T(8,128)(2,1)} %get-tuple-element.8) | data formatting | bytes 262144
  130.8 1.9 %copy.11 = bf16[1,2048,128]{2,1,0:T(8,128)(2,1)} copy(bf16[1,2048,128]{2,1,0:T(8,128)(2,1)} %bitcast.2) | data formatting | bytes 1048576
